TPU v7x, 512 devices: a whole 4x4x16 slice. The times are simulated.
512 devices in a mesh: expert: 64 (over z_lo, y, core), tensor: 8 (over x, z_hi).
Axes of the slice: x: 4, y: 4, z: 16 (z_hi: 2, z_lo: 8; z = z_hi * 8 + z_lo), core: 2. Of those that a mesh axis runs over, the one named last changes fastest.
Arguments:
- tokens: bfloat16 [8192, 2048], P('expert', 'tensor'), may hold values from -6 to 6
- upstream: bfloat16 [8192, 2048], P('expert', 'tensor'), may hold values from -6 to 6
- probs: bfloat16 [8192, 6], P('expert'), may hold values from 0.049804688 to 1
- expert_ids: int32 [8192, 6], P('expert'), may hold values from 0 to 63, all different within a row; in each aligned block of 128 rows (0 to 127, 128 to 255, ...) at most 16 rows name the same one
- gate_weight: bfloat16 [64, 1408, 2048], P('expert', 'tensor'), may hold values from -0.125 to 0.125
- up_weight: bfloat16 [64, 1408, 2048], P('expert', 'tensor'), may hold values from -0.125 to 0.125
- down_weight: bfloat16 [64, 1408, 2048], P('expert', 'tensor'), may hold values from -0.15625 to 0.15625
Outputs:
- grad_tokens: bfloat16 [8192, 2048], P('expert', 'tensor')
- grad_probs: bfloat16 [8192, 6], P('expert')
- grad_gate: bfloat16 [64, 1408, 2048], P('expert', 'tensor')
- grad_up: bfloat16 [64, 1408, 2048], P('expert', 'tensor')
- grad_down: bfloat16 [64, 1408, 2048], P('expert', 'tensor')
Inputs may be any that keep to these rules, and one draw needn't show every extreme that they name: `expert_ids`: each token names 6 different experts. Among the 128 tokens of one aligned block no expert is named more than 16 times, and in every draw some expert is named exactly 16 times in some block; every expert is named by some token.
All inputs are finite; a program needn't handle non-finite values.
Results may differ from a plain program's by a relative error of at most 0.018.
Values may be sent and summed in bfloat16 or wider, within the bound.
A program may use at most 64 MiB of HBM per device.

v0:
```python
import jax
import jax.numpy as jnp
from jax import lax
from jax.sharding import PartitionSpec as P


def contract(left, right, left_dim, right_dim):
    return lax.dot_general(
        left, right, (((left_dim,), (right_dim,)), ((), ())), preferred_element_type=jnp.float32
    )


def body(tokens, upstream, probs, expert_ids, gate_weight, up_weight, down_weight):
    tok_rows, top = expert_ids.shape
    experts = gate_weight.shape[0] * lax.axis_size("expert")
    capacity = 4 * top * tok_rows // (3 * experts)
    flat_ids = expert_ids.reshape(-1)
    onehot = (flat_ids[:, None] == jnp.arange(experts, dtype=jnp.int32)[None, :]).astype(jnp.int32)
    before = jnp.cumsum(onehot, axis=0) - onehot
    slot = jnp.sum(before * onehot, axis=1)
    dest = flat_ids * capacity + slot
    count = tok_rows * top
    owner = jnp.full((experts * capacity,), count, jnp.int32)
    owner = owner.at[dest].set(jnp.arange(count, dtype=jnp.int32))
    source_tok = owner // top
    prob_rows = jnp.concatenate([probs.reshape(-1), jnp.zeros((1,), jnp.bfloat16)], axis=0)[owner]
    prob_rows = prob_rows.reshape(experts, capacity)

    def pack(values):
        padded = jnp.concatenate([values, jnp.zeros((1, values.shape[1]), values.dtype)], axis=0)
        return padded[source_tok].reshape(experts, capacity, values.shape[1])

    whole_x, whole_dy = (
        lax.all_gather(tokens, "tensor", axis=1, tiled=True),
        lax.all_gather(upstream, "tensor", axis=1, tiled=True),
    )
    x_in, dy_in, p_in = (
        lax.all_to_all(pack(whole_x), "expert", split_axis=0, concat_axis=0, tiled=True),
        lax.all_to_all(pack(whole_dy), "expert", split_axis=0, concat_axis=0, tiled=True),
        lax.all_to_all(prob_rows, "expert", split_axis=0, concat_axis=0, tiled=True),
    )
    sources = x_in.shape[0]
    width = x_in.shape[2]
    total_rows = sources * capacity
    xs = x_in.reshape(total_rows, width)
    dys = dy_in.reshape(total_rows, width)
    weight = p_in.reshape(total_rows).astype(jnp.float32)
    w_gate = gate_weight[0]
    w_up = up_weight[0]
    w_down = down_weight[0]
    a = contract(xs, w_gate, 1, 1)
    u = contract(xs, w_up, 1, 1)
    sig = jax.nn.sigmoid(a)
    act = a * sig
    hidden = (act * u).astype(jnp.bfloat16)
    g = contract(dys, w_down, 1, 1)
    partial_dp = jnp.sum(hidden.astype(jnp.float32) * g, axis=1)
    dh = weight[:, None] * g
    d_a = (dh * u * sig * (1.0 + a * (1.0 - sig))).astype(jnp.bfloat16)
    d_u = (dh * act).astype(jnp.bfloat16)
    dx_part = contract(d_a, w_gate, 1, 0) + contract(d_u, w_up, 1, 0)
    dx_rows = lax.psum_scatter(
        dx_part.reshape(sources, capacity, width).astype(jnp.bfloat16),
        "tensor",
        scatter_dimension=2,
        tiled=True,
    )
    dp_rows = lax.psum(partial_dp, "tensor").astype(jnp.bfloat16).reshape(sources, capacity)
    grad_gate = contract(d_a, xs, 0, 0).astype(jnp.bfloat16)
    grad_up = contract(d_u, xs, 0, 0).astype(jnp.bfloat16)
    scaled = (weight[:, None] * hidden.astype(jnp.float32)).astype(jnp.bfloat16)
    grad_down = contract(scaled, dys, 0, 0).astype(jnp.bfloat16)
    back_x, back_p = (
        lax.all_to_all(dx_rows, "expert", split_axis=0, concat_axis=0, tiled=True),
        lax.all_to_all(dp_rows, "expert", split_axis=0, concat_axis=0, tiled=True),
    )
    local_width = back_x.shape[2]
    picked = back_x.reshape(experts * capacity, local_width)[dest].reshape(
        tok_rows, top, local_width
    )
    grad_tokens = jnp.sum(picked.astype(jnp.float32), axis=1).astype(jnp.bfloat16)
    grad_probs = back_p.reshape(-1)[dest].reshape(tok_rows, top)
    return (grad_tokens, grad_probs, grad_gate[None], grad_up[None], grad_down[None])


def solution(mesh):
    placed = (
        P("expert", "tensor"),
        P("expert", "tensor"),
        P("expert", None),
        P("expert", None),
        P("expert", "tensor", None),
        P("expert", "tensor", None),
        P("expert", "tensor", None),
    )
    return jax.shard_map(
        body,
        mesh=mesh,
        in_specs=placed,
        out_specs=(
            P("expert", "tensor"),
            P("expert", None),
            P("expert", "tensor", None),
            P("expert", "tensor", None),
            P("expert", "tensor", None),
        ),
        check_vma=False,
    )
```

profile of v0, /device:TPU:1, one launch (start us, length us, event | category | flops | bytes accessed | tf_op | source)
XLA Modules:
  0.0 859.5 jit_solution(16834652398656970523)
XLA Ops:
  7.2 0.8 broadcast_multiply_fusion
  7.9 0.8 copy.20
  9.0 0.8 copy.18
  10.3 1.8 reduce-window.6
  12.5 3.4 scatter_custom_fusion
  16.0 6.8 gather_fusion
  22.8 0.7 all_to_all.28
  23.5 17.2 %all-to-all-start = ((bf16[64,1,16]{2,1,0:T(2,128)(2,1)}), bf16[64,1,16]{2,1,0:T(2,128)(2,1)S(1)}, u32[]{:S(2)}, u32[]{:S(2)}) async-start(bf16[64,1,16]{2,1,0:T(2,128)(2,1)} %all_to_all.28), calls=%async_computation | async-start | bytes 65536 | tf_op jit(solution)/shard_map/all_to_all | solution.py:40
  40.7 77.4 %all_gather.7 = bf16[128,2048]{1,0:T(8,128)(2,1)S(1)} all-gather(bf16[128,256]{1,0:T(8,128)(2,1)} %param.7), channel_id=1, replica_groups=mesh['expert'=64,'tensor'=8] {'tensor'}, dimensions={1}, use_global_device_ids=true | all-gather | bytes 589824 | tf_op jit(solution)/shard_map/all_gather | solution.py:34
  118.1 6.0 gather_fusion.2
  124.2 17.3 %all-to-all-start.2 = ((bf16[64,16,2048]{2,1,0:T(8,128)(2,1)}), bf16[64,16,2048]{2,1,0:T(8,128)(2,1)}, u32[]{:S(2)}, u32[]{:S(2)}) async-start(bf16[64,16,2048]{2,1,0:T(8,128)(2,1)} %bitcast.60), calls=%async_computation.2 | async-start | bytes 8388608 | tf_op jit(solution)/shard_map/all_to_all | solution.py:38
  141.4 140.2 %all_gather.6 = bf16[128,2048]{1,0:T(8,128)(2,1)S(1)} all-gather(bf16[128,256]{1,0:T(8,128)(2,1)S(1)} %copy-done.2), channel_id=1, replica_groups=mesh['expert'=64,'tensor'=8] {'tensor'}, dimensions={1}, use_global_device_ids=true | all-gather | bytes 589824 | tf_op jit(solution)/shard_map/all_gather | solution.py:35
  281.7 6.1 gather_fusion.1
  287.8 71.5 %all-to-all-done.2 = bf16[64,16,2048]{2,1,0:T(8,128)(2,1)} async-done(((bf16[64,16,2048]{2,1,0:T(8,128)(2,1)}), bf16[64,16,2048]{2,1,0:T(8,128)(2,1)}, u32[]{:S(2)}, u32[]{:S(2)}) %all-to-all-start.2) | async-done | bytes 4194336 | tf_op jit(solution)/shard_map/all_to_all | solution.py:38
  359.3 54.4 %all-to-all-start.1 = ((bf16[64,16,2048]{2,1,0:T(8,128)(2,1)}), bf16[64,16,2048]{2,1,0:T(8,128)(2,1)}, u32[]{:S(2)}, u32[]{:S(2)}) async-start(bf16[64,16,2048]{2,1,0:T(8,128)(2,1)} %bitcast.59), calls=%async_computation.1 | async-start | bytes 8388608 | tf_op jit(solution)/shard_map/all_to_all | solution.py:39
  414.1 4.6 fusion.7
  418.7 4.7 fusion.10
  423.3 176.1 %all-to-all-done.1 = bf16[64,16,2048]{2,1,0:T(8,128)(2,1)} async-done(((bf16[64,16,2048]{2,1,0:T(8,128)(2,1)}), bf16[64,16,2048]{2,1,0:T(8,128)(2,1)}, u32[]{:S(2)}, u32[]{:S(2)}) %all-to-all-start.1) | async-done | bytes 4194336 | tf_op jit(solution)/shard_map/all_to_all | solution.py:39
  599.4 4.4 fusion.3
  603.8 1.3 fusion.5
  605.1 3.3 add_convert_fusion
  608.4 36.6 %psum.7 = bf16[1024]{0:T(1024)(128)(2,1)S(1)} all-reduce(f32[1024]{0:T(1024)S(1)} %get-tuple-element.15), channel_id=1, replica_groups=mesh['expert'=64,'tensor'=8] {'tensor'}, use_global_device_ids=true, to_apply=%region_7.8 | all-reduce | flops 1024 | bytes 6144 | tf_op jit(solution)/shard_map/psum | solution.py:68
  645.1 36.5 %all_to_all.35 = bf16[64,1,16]{2,1,0:T(2,128)(2,1)S(1)} all-to-all(bf16[64,1,16]{2,1,0:T(2,128)(2,1)S(1)} %all_to_all.29), channel_id=1, replica_groups=mesh['expert'=64,'tensor'=8] {'expert'}, dimensions={0} | all-to-all | bytes 4096 | tf_op jit(solution)/shard_map/all_to_all | solution.py:75
  681.7 130.2 %reduce-scatter.2.cloned.1.call-done = bf16[64,16,256]{2,1,0:T(8,128)(2,1)} async-done(((bf16[64,16,2048]{2,1,0:T(8,128)(2,1)}), bf16[64,16,256]{2,1,0:T(8,128)(2,1)}) %reduce-scatter.2.cloned.1.call-update) | async-done | bytes 524304 | tf_op jit(solution)/shard_map/reduce_scatter | solution.py:62
  811.9 6.9 all-to-all-start.3
  818.8 4.0 fusion
  822.8 4.0 fusion.1
  826.7 4.0 fusion.2
  830.9 5.0 gather_fusion.4
  836.7 12.2 %all-to-all-done.3 = bf16[64,16,256]{2,1,0:T(8,128)(2,1)S(1)} async-done(((bf16[64,16,256]{2,1,0:T(8,128)(2,1)}), bf16[64,16,256]{2,1,0:T(8,128)(2,1)S(1)}, u32[]{:S(2)}, u32[]{:S(2)}) %all-to-all-start.3) | async-done | bytes 524320 | tf_op jit(solution)/shard_map/all_to_all | solution.py:74
  848.9 2.6 gather_fusion.3
  851.7 1.0 reduce_sum.34
  (35 shorter events, 2.9 us)
Async XLA Ops:
  7.2 406.9 %copy-start = (bf16[1,176,2048]{2,1,0:T(8,128)(2,1)S(1)}, bf16[1,176,2048]{2,1,0:T(8,128)(2,1)}, u32[]{:S(2)}) copy-start(bf16[1,176,2048]{2,1,0:T(8,128)(2,1)} %param.11) | copy-start | bytes 2162692
  23.5 100.7 %all-to-all-start = ((bf16[64,1,16]{2,1,0:T(2,128)(2,1)}), bf16[64,1,16]{2,1,0:T(2,128)(2,1)S(1)}, u32[]{:S(2)}, u32[]{:S(2)}) async-start(bf16[64,1,16]{2,1,0:T(2,128)(2,1)} %all_to_all.28), calls=%async_computation | async-start | bytes 65536 | tf_op jit(solution)/shard_map/all_to_all | solution.py:40
  124.2 17.3 %copy-start.2 = (bf16[128,256]{1,0:T(8,128)(2,1)S(1)}, bf16[128,256]{1,0:T(8,128)(2,1)}, u32[]{:S(2)}) copy-start(bf16[128,256]{1,0:T(8,128)(2,1)} %param.8) | copy-start | bytes 196612
  124.2 235.1 %all-to-all-start.2 = ((bf16[64,16,2048]{2,1,0:T(8,128)(2,1)}), bf16[64,16,2048]{2,1,0:T(8,128)(2,1)}, u32[]{:S(2)}, u32[]{:S(2)}) async-start(bf16[64,16,2048]{2,1,0:T(8,128)(2,1)} %bitcast.60), calls=%async_computation.2 | async-start | bytes 8388608 | tf_op jit(solution)/shard_map/all_to_all | solution.py:38
  359.3 240.1 %all-to-all-start.1 = ((bf16[64,16,2048]{2,1,0:T(8,128)(2,1)}), bf16[64,16,2048]{2,1,0:T(8,128)(2,1)}, u32[]{:S(2)}, u32[]{:S(2)}) async-start(bf16[64,16,2048]{2,1,0:T(8,128)(2,1)} %bitcast.59), calls=%async_computation.1 | async-start | bytes 8388608 | tf_op jit(solution)/shard_map/all_to_all | solution.py:39
  413.6 5.0 copy-start.1
  413.7 398.2 %reduce-scatter.2.cloned.1.call-start = ((), (), s32[]{:S(2)}) async-start(), calls=%async_computation.6 | async-start | bytes 4718592 | tf_op jit(solution)/shard_map/reduce_scatter | solution.py:62
  418.7 180.8 %copy-start.3 = (bf16[1,176,2048]{2,1,0:T(8,128)(2,1)S(1)}, bf16[1,176,2048]{2,1,0:T(8,128)(2,1)}, u32[]{:S(2)}) copy-start(bf16[1,176,2048]{2,1,0:T(8,128)(2,1)} %param.13) | copy-start | bytes 2162692
  811.9 37.0 %all-to-all-start.3 = ((bf16[64,16,256]{2,1,0:T(8,128)(2,1)}), bf16[64,16,256]{2,1,0:T(8,128)(2,1)S(1)}, u32[]{:S(2)}, u32[]{:S(2)}) async-start(bf16[64,16,256]{2,1,0:T(8,128)(2,1)} %reduce-scatter.2.cloned.1.call-done), calls=%async_computation.4 | async-start | bytes 1048576 | tf_op jit(solution)/shard_map/all_to_all | solution.py:74
Sparse Core Ops, SparseCore 0:
  608.6 203.2 reduce-scatter.1
where the time goes:
time: 860 us
  waiting for transfers between devices  390 us (45%)
  blocking collectives  291 us (34%)
  starting transfers between devices  95.9 us (11%)
  local copies, waits for them, and re-layouts  34.5 us (4%)
  matrix products  30.2 us (4%)
  between operations  14.3 us (2%)
    all_to_all x1, waiting for transfers between devices, body(): lax.all_to_all(pack(whole_dy), 'expert', split_axis=0, concat_axis=0, til...  176 us
    all_gather x1, blocking collectives, body(): lax.all_gather(upstream, 'tensor', axis=1, tiled=True)  140 us
    reduce_scatter x1, waiting for transfers between devices, body(): lax.psum_scatter(dx_part.reshape(sources, capacity, width).astype(jnp.bfl...  130 us
    all_gather x1, blocking collectives, body(): lax.all_gather(tokens, 'tensor', axis=1, tiled=True)  77.4 us
    all_to_all x1, waiting for transfers between devices, body(): lax.all_to_all(pack(whole_x), 'expert', split_axis=0, concat_axis=0, tile...  71.5 us
    all_to_all x1, starting transfers between devices, body(): lax.all_to_all(pack(whole_dy), 'expert', split_axis=0, concat_axis=0, til...  54.4 us
    psum x1, blocking collectives, body(): lax.psum(partial_dp, 'tensor').astype(jnp.bfloat16)  36.6 us
    all_to_all x1, blocking collectives, body(): lax.all_to_all(dp_rows, 'expert', split_axis=0, concat_axis=0, tiled=True)  36.5 us
  transfers between devices with their start and end apart: 5, of which 4 were waited for; matrix products, arithmetic and copies ran while one was open for 5% of the time, Pallas kernels for 0%

commit v1 on v0

v1 whole, which is shorter than its diff:
```python
import jax
import jax.numpy as jnp
from jax import lax
from jax.experimental import pallas as pl
from jax.experimental.pallas import tpu as pltpu
from jax.sharding import Mesh
from jax.sharding import PartitionSpec as P

MESH = pl.DeviceIdType.MESH
F32 = jnp.float32
BF16 = jnp.bfloat16

ZL, NY, NC, NX, ZH = 8, 4, 2, 4, 2
NZ = ZL * ZH
YC = NY * NC
TOK = 128
TOP = 6
CAP = 16
FS = 256
HID = 176
META = 16
WIDE = 2 * FS
HALF = TOK // 2


def dot(a, b, ad=1, bd=0):
    return lax.dot_general(a, b, (((ad,), (bd,)), ((), ())), preferred_element_type=F32)


def arrived(ref, sem):
    pltpu.make_async_copy(ref, ref, sem).wait()


def kernel(
    tok, ups, prob, ids, wg, wu, wd,
    gtok, gprob, ggate, gup, gdown,
    held, ysend, wsend, rows_x, wrow, dau_t, ph_t, own, part_o, part_rl, buf_a, buf_b,
    fsend, frecv, gsend, zrecv, dpx,
    s_z, r_z, s_y, r_y, s_w, r_w, s_x, r_x, s_a, r_a, s_b, r_b, s_f, r_f, s_g, r_g, s_d, r_d,
):
    zl, zh = lax.axis_index("zl"), lax.axis_index("zh")
    x = lax.axis_index("x")
    me = lax.axis_index("y") * NC + lax.axis_index("c")
    z = zh * ZL + zl

    def at_z(place):
        return {"zl": lax.rem(place, ZL), "zh": lax.div(place, ZL)}

    def at_yc(place):
        return {"y": lax.div(place, NC), "c": lax.rem(place, NC)}

    right, left = {"x": lax.rem(x + 1, NX)}, {"x": lax.rem(x + 3, NX)}

    def send(src, dst, s_sem, r_sem, device):
        pltpu.make_async_remote_copy(
            src_ref=src, dst_ref=dst, send_sem=s_sem, recv_sem=r_sem,
            device_id=device, device_id_type=MESH,
        ).start()

    barrier = pltpu.get_barrier_semaphore()
    for d in range(1, NZ):
        pl.semaphore_signal(barrier, inc=1, device_id=at_z(lax.rem(z + d, NZ)), device_id_type=MESH)
    for d in range(1, YC):
        pl.semaphore_signal(barrier, inc=1, device_id=at_yc(lax.rem(me + d, YC)), device_id_type=MESH)
    for d in range(1, NX):
        pl.semaphore_signal(barrier, inc=1, device_id={"x": lax.rem(x + d, NX)}, device_id_type=MESH)

    row_id = lax.broadcasted_iota(jnp.int32, (TOK, TOK), 0)
    col_id = lax.broadcasted_iota(jnp.int32, (TOK, TOK), 1)
    eye = (row_id == col_id).astype(F32).astype(BF16)
    earlier = (row_id < col_id).astype(F32).astype(BF16)
    held[0, 0:TOK, 0:FS] = tok[...]
    held[0, 0:TOK, FS:WIDE] = ups[...]
    ids_t = dot(ids[...].astype(F32).astype(BF16), eye, 0, 0)
    prob_t = dot(prob[...], eye, 0, 0)
    expert = lax.broadcasted_iota(jnp.int32, (ZL * YC, TOK), 0).astype(F32)
    named = jnp.zeros((ZL * YC, TOK), F32)
    for k in range(TOP):
        named = named + jnp.where(ids_t[k : k + 1] == expert, 1.0, 0.0)
    before = dot(named.astype(BF16), earlier)
    line = lax.broadcasted_iota(jnp.int32, (META, TOK), 0)
    id_rows = jnp.zeros((META, TOK), F32)
    slot_rows = jnp.zeros((META, TOK), F32)
    prob_rows = jnp.zeros((META, TOK), F32)
    for k in range(TOP):
        slot = jnp.sum(jnp.where(ids_t[k : k + 1] == expert, before, 0.0), axis=0, keepdims=True)
        id_rows = jnp.where(line == k, ids_t[k : k + 1], id_rows)
        slot_rows = jnp.where(line == k, slot, slot_rows)
        prob_rows = jnp.where(line == k, prob_t[k : k + 1], prob_rows)
    held[0, TOK : TOK + META, 0:TOK] = id_rows.astype(BF16)
    held[0, TOK : TOK + META, TOK : 2 * TOK] = slot_rows.astype(BF16)
    held[0, TOK : TOK + META, 2 * TOK : 3 * TOK] = prob_rows.astype(BF16)
    held[0, TOK : TOK + META, 3 * TOK : 4 * TOK] = jnp.zeros((META, TOK), BF16)

    pl.semaphore_wait(barrier, NZ + YC + NX - 3)

    def source(p):
        odd = lax.rem(p, 2) == 1
        place = lax.rem(z + jnp.where(odd, NZ - lax.div(p + 1, 2), lax.div(p, 2)), NZ)
        return lax.rem(place, ZL), lax.div(place, ZL)

    def block_rows(block, count=TOK, extra=0):
        return pl.ds(pl.multiple_of(block * TOK + extra, CAP), count)

    row_f = row_id.astype(F32)

    def routing(p):
        meta = held[p, TOK : TOK + META, :].astype(F32)
        code = (meta[:, 0:TOK] - (zl * YC).astype(F32)) * CAP + meta[:, TOK : 2 * TOK]
        return code, meta[:, 2 * TOK : 3 * TOK]

    def spread(code, values):
        total = jnp.zeros((TOK, TOK), F32)
        for k in range(TOP):
            value = 1.0 if values is None else values[k : k + 1]
            total = total + jnp.where(row_f == code[k : k + 1], value, 0.0)
        return total

    def take_in(p):
        @pl.when(p > 0)
        def _():
            arrived(held.at[p], r_z.at[p])

        @pl.when(p == 0)
        def _():
            send(held.at[0], held.at[1], s_z, r_z.at[1], at_z(lax.rem(z + 1, NZ)))
            send(held.at[0], held.at[2], s_z, r_z.at[2], at_z(lax.rem(z + NZ - 1, NZ)))

        @pl.when((p > 0) & (p < NZ - 2))
        def _():
            step = jnp.where(lax.rem(p, 2) == 1, 1, NZ - 1)
            send(held.at[p], held.at[p + 2], s_z, r_z.at[p + 2], at_z(lax.rem(z + step, NZ)))

        block, half = source(p)
        code, weights = routing(p)
        pick = spread(code, None).astype(BF16)
        ysend[p] = dot(pick, held[p, 0:TOK, :]).astype(BF16)
        mine = block_rows(block, CAP, me * CAP)
        my_rows = pl.ds(pl.multiple_of(me * CAP, CAP), CAP)
        rows_x[0, half, mine, :] = ysend[p, my_rows, :]
        for d in range(1, YC):
            to = lax.rem(me + d, YC)
            theirs = pl.ds(pl.multiple_of(to * CAP, CAP), CAP)
            send(ysend.at[p, theirs, :], rows_x.at[0, half, mine, :], s_y, r_y.at[p], at_yc(to))

        @pl.when(p >= ZL)
        def _():
            q = p - ZL
            weight = jnp.sum(spread(code, weights), axis=1, keepdims=True)
            wsend[q] = jnp.broadcast_to(weight, (TOK, TOK)).astype(BF16)
            wrow[mine, :] = wsend[q, my_rows, :]
            for d in range(1, YC):
                to = lax.rem(me + d, YC)
                theirs = pl.ds(pl.multiple_of(to * CAP, CAP), CAP)
                send(wsend.at[q, theirs, :], wrow.at[mine, :], s_w, r_w.at[q], at_yc(to))

    def pass_on(p):
        block, half = source(p)
        rows = block_rows(block)
        arrived(ysend.at[p, pl.ds(0, TOK - CAP), :], r_y.at[p])

        @pl.when(p >= ZL)
        def _():
            arrived(wsend.at[p - ZL, pl.ds(0, TOK - CAP), :], r_w.at[p - ZL])

        send(rows_x.at[0, half, rows, :], rows_x.at[1, half, rows, :], s_x, r_x.at[p, 0], right)
        send(rows_x.at[0, half, rows, :], rows_x.at[2, half, rows, :], s_x, r_x.at[p, 1], left)

    def relay(p):
        block, half = source(p)
        rows = block_rows(block)
        low, high = block_rows(block, HALF), block_rows(block, HALF, HALF)
        arrived(rows_x.at[1, half, rows, :], r_x.at[p, 0])
        send(rows_x.at[1, half, low, :], rows_x.at[3, half, low, :], s_x, r_x.at[p, 2], right)
        arrived(rows_x.at[2, half, rows, :], r_x.at[p, 1])
        send(rows_x.at[2, half, high, :], rows_x.at[3, half, high, :], s_x, r_x.at[p, 3], left)

    def all_here(p):
        block, half = source(p)
        arrived(rows_x.at[3, half, block_rows(block, HALF), :], r_x.at[p, 2])
        arrived(rows_x.at[3, half, block_rows(block, HALF, HALF), :], r_x.at[p, 3])

    def features(slot, half):
        shift = (0, 3, 1, 2)[slot] if isinstance(slot, int) else jnp.where(
            slot == 0, 0, jnp.where(slot == 1, 3, slot - 1)
        )
        return pl.ds(pl.multiple_of((lax.rem(x + shift, NX) * ZH + half) * FS, FS), FS)

    def compute(p):
        q = p - ZL
        block, _ = source(p)
        rows = block_rows(block)
        a = jnp.zeros((TOK, HID), F32)
        u = jnp.zeros((TOK, HID), F32)
        g = jnp.zeros((TOK, HID), F32)
        for slot in range(NX):
            for half in range(ZH):
                f = features(slot, half)
                xs = rows_x[slot, half, rows, 0:FS]
                dys = rows_x[slot, half, rows, FS:WIDE]
                a = a + dot(xs, wg[0, :, f], 1, 1)
                u = u + dot(xs, wu[0, :, f], 1, 1)
                g = g + dot(dys, wd[0, :, f], 1, 1)
        weight = wrow[rows, :].astype(F32)[:, 0:1]
        sig = jax.nn.sigmoid(a)
        act = a * sig
        hidden = (act * u).astype(BF16).astype(F32)
        dp = jnp.sum(hidden * g, axis=1, keepdims=True)
        fsend[q, :, WIDE : WIDE + TOK] = jnp.broadcast_to(dp, (TOK, TOK)).astype(BF16)
        dh = weight * g
        d_a = dh * u * sig * (1.0 + a * (1.0 - sig))
        d_u = dh * act
        lanes = pl.ds(pl.multiple_of(block * TOK, TOK), TOK)
        dau_t[0:HID, lanes] = d_a.T.astype(BF16)
        dau_t[HID : 2 * HID, lanes] = d_u.T.astype(BF16)
        ph_t[:, lanes] = (weight * hidden).T.astype(BF16)
        d_a = d_a.astype(BF16)
        d_u = d_u.astype(BF16)
        for slot in (3, 2, 1, 0):
            for half in range(ZH):
                f = features(slot, half)
                to = slice(half * FS, half * FS + FS)
                term = dot(d_a, wg[0, :, f]) + dot(d_u, wu[0, :, f])
                if slot == 0:
                    own[q, :, to] = term
                elif slot == 3:
                    part_o[q, :, to] = term.astype(BF16)
                else:
                    part_rl[2 - slot, q, :, to] = term.astype(BF16)
            if slot == 3:
                send(part_o.at[q, pl.ds(0, HALF), :], buf_a.at[0, q], s_a, r_a.at[q, 0], right)
                send(part_o.at[q, pl.ds(HALF, HALF), :], buf_a.at[1, q], s_a, r_a.at[q, 1], left)

    def add_relay(p):
        q = p - ZL
        arrived(buf_a.at[0, q], r_a.at[q, 0])
        part_rl[0, q, 0:HALF, :] = (
            part_rl[0, q, 0:HALF, :].astype(F32) + buf_a[0, q].astype(F32)
        ).astype(BF16)
        send(part_rl.at[0, q], buf_b.at[0, q], s_b, r_b.at[q, 0], right)
        arrived(buf_a.at[1, q], r_a.at[q, 1])
        part_rl[1, q, HALF:TOK, :] = (
            part_rl[1, q, HALF:TOK, :].astype(F32) + buf_a[1, q].astype(F32)
        ).astype(BF16)
        send(part_rl.at[1, q], buf_b.at[1, q], s_b, r_b.at[q, 1], left)

    def send_back(p):
        q = p - ZL
        arrived(buf_b.at[0, q], r_b.at[q, 0])
        arrived(buf_b.at[1, q], r_b.at[q, 1])
        fsend[q, :, 0:WIDE] = (
            own[q] + buf_b[0, q].astype(F32) + buf_b[1, q].astype(F32)
        ).astype(BF16)
        my_rows = pl.ds(pl.multiple_of(me * CAP, CAP), CAP)
        frecv[q, my_rows, :] = fsend[q, my_rows, :]
        for d in range(1, YC):
            to = lax.rem(me + d, YC)
            theirs = pl.ds(pl.multiple_of(to * CAP, CAP), CAP)
            send(fsend.at[q, theirs, :], frecv.at[q, my_rows, :], s_f, r_f.at[q], at_yc(to))

    def combine(p):
        q = p - ZL
        block, _ = source(p)
        arrived(fsend.at[q, pl.ds(0, TOK - CAP), :], r_f.at[q])
        code, _ = routing(p)
        pick = spread(code, None).astype(BF16)
        total = dot(pick, frecv[q, :, 0:WIDE], 0, 0).astype(BF16)
        dp = frecv[q, :, WIDE : WIDE + TOK].astype(F32)
        dp_rows = jnp.zeros((META, TOK), F32)
        for k in range(TOP):
            one = jnp.sum(jnp.where(row_f == code[k : k + 1], dp, 0.0), axis=0, keepdims=True)
            dp_rows = jnp.where(line == k, one, dp_rows)
        for half in range(ZH):
            gsend[q, half, 0:TOK, :] = total[:, half * FS : half * FS + FS]
            gsend[q, half, TOK : TOK + META, 0:TOK] = dp_rows.astype(BF16)
            gsend[q, half, TOK : TOK + META, TOK : 2 * TOK] = jnp.zeros((META, TOK), BF16)

        @pl.when(q < ZL - 1)
        def _():
            for half in range(ZH):
                to = block + half * ZL
                send(gsend.at[q, half], zrecv.at[lax.rem(to + NZ - z, NZ)], s_g, r_g, at_z(to))

        @pl.when(q == ZL - 1)
        def _():
            zrecv[0] = gsend[ZL - 1, zh]
            send(gsend.at[ZL - 1, 1 - zh], zrecv.at[ZL], s_g, r_g, at_z(lax.rem(z + ZL, NZ)))

    def weight_grads(slot):
        for half in range(ZH):
            f = features(slot, half)
            both = dot(dau_t[...], rows_x[slot, half, :, 0:FS])
            ggate[0, :, f] = both[0:HID].astype(BF16)
            gup[0, :, f] = both[HID : 2 * HID].astype(BF16)
            gdown[0, :, f] = dot(ph_t[...], rows_x[slot, half, :, FS:WIDE]).astype(BF16)

    def step(i, carry):
        def when(lag, least, act):
            p = i - lag

            @pl.when((p >= least) & (p < NZ))
            def _():
                act(p)

        when(0, 0, take_in)
        when(1, 0, pass_on)
        when(2, 0, relay)
        when(6, ZL, combine)
        when(5, ZL, send_back)
        when(4, ZL, add_relay)
        when(3, 0, all_here)
        when(3, ZL, compute)

        @pl.when(i >= NZ + 2)
        def _():
            weight_grads(i - (NZ + 2))

        return carry

    lax.fori_loop(0, NZ + 6, step, 0)

    arrived(zrecv.at[pl.ds(1, NZ - 1)], r_g)
    total = jnp.zeros((TOK, FS), F32)
    dp = jnp.zeros((META, TOK), F32)
    for s in range(NZ):
        total = total + zrecv[s, 0:TOK, :].astype(F32)
        dp = dp + zrecv[s, TOK : TOK + META, 0:TOK].astype(F32)
    dpx[x] = dp
    for d in range(1, NX):
        send(dpx.at[x], dpx.at[x], s_d, r_d, {"x": lax.rem(x + d, NX)})
    gtok[...] = total.astype(BF16)
    arrived(dpx.at[pl.ds(0, NX - 1)], r_d)
    dp = (dpx[0] + dpx[1]) + (dpx[2] + dpx[3])
    gprob[...] = dot(eye, dp.astype(BF16), 1, 1)[:, 0:TOP].astype(BF16)

    arrived(held.at[pl.ds(0, NZ - 1)], s_z)
    arrived(ysend.at[:, pl.ds(0, TOK - CAP), :], s_y)
    arrived(wsend.at[:, pl.ds(0, TOK - CAP), :], s_w)
    arrived(rows_x.at[pl.ds(1, NX - 1)], s_x)
    arrived(part_o, s_a)
    arrived(part_rl, s_b)
    arrived(fsend.at[:, pl.ds(0, TOK - CAP), :], s_f)
    arrived(zrecv.at[pl.ds(1, NZ - 1)], s_g)
    arrived(dpx.at[pl.ds(0, NX - 1)], s_d)


def body(tokens, upstream, probs, expert_ids, gate_weight, up_weight, down_weight):
    vmem = pl.BlockSpec(memory_space=pltpu.VMEM)
    dma = pltpu.SemaphoreType.DMA
    width = NX * ZH * FS
    out = (
        jax.ShapeDtypeStruct((TOK, FS), BF16),
        jax.ShapeDtypeStruct((TOK, TOP), BF16),
    ) + (jax.ShapeDtypeStruct((1, HID, width), BF16),) * 3
    return pl.pallas_call(
        kernel,
        out_shape=out,
        in_specs=[vmem] * 7,
        out_specs=(vmem,) * 5,
        scratch_shapes=[
            pltpu.VMEM((NZ, TOK + META, WIDE), BF16),
            pltpu.VMEM((NZ, TOK, WIDE), BF16),
            pltpu.VMEM((ZL, TOK, TOK), BF16),
            pltpu.VMEM((NX, ZH, ZL * TOK, WIDE), BF16),
            pltpu.VMEM((ZL * TOK, TOK), BF16),
            pltpu.VMEM((2 * HID, ZL * TOK), BF16),
            pltpu.VMEM((HID, ZL * TOK), BF16),
            pltpu.VMEM((ZL, TOK, WIDE), F32),
            pltpu.VMEM((ZL, TOK, WIDE), BF16),
            pltpu.VMEM((2, ZL, TOK, WIDE), BF16),
            pltpu.VMEM((2, ZL, HALF, WIDE), BF16),
            pltpu.VMEM((2, ZL, TOK, WIDE), BF16),
            pltpu.VMEM((ZL, TOK, WIDE + TOK), BF16),
            pltpu.VMEM((ZL, TOK, WIDE + TOK), BF16),
            pltpu.VMEM((ZL, ZH, TOK + META, FS), BF16),
            pltpu.VMEM((NZ, TOK + META, FS), BF16),
            pltpu.VMEM((NX, META, TOK), F32),
            dma, dma((NZ,)),
            dma, dma((NZ,)),
            dma, dma((ZL,)),
            dma, dma((NZ, 4)),
            dma, dma((ZL, 2)),
            dma, dma((ZL, 2)),
            dma, dma((ZL,)),
            dma, dma,
            dma, dma,
        ],
        compiler_params=pltpu.CompilerParams(
            collective_id=0, has_side_effects=True, vmem_limit_bytes=56 * 1024 * 1024
        ),
        cost_estimate=pl.CostEstimate(
            flops=16 * ZL * TOK * HID * width, bytes_accessed=8 << 20, transcendentals=0
        ),
    )(tokens, upstream, probs, expert_ids, gate_weight, up_weight, down_weight)


def solution(mesh):
    parts = Mesh(mesh.devices.reshape(ZL, NY, NC, NX, ZH), ("zl", "y", "c", "x", "zh"))
    expert, tensor = ("zl", "y", "c"), ("x", "zh")
    placed = (
        P(expert, tensor),
        P(expert, tensor),
        P(expert, None),
        P(expert, None),
        P(expert, tensor, None),
        P(expert, tensor, None),
        P(expert, tensor, None),
    )
    return jax.shard_map(
        body,
        mesh=parts,
        in_specs=placed,
        out_specs=(
            P(expert, tensor),
            P(expert, None),
            P(expert, tensor, None),
            P(expert, tensor, None),
            P(expert, tensor, None),
        ),
        check_vma=False,
    )
```

time: 860 us -> 172 us (0.20)
  waiting for transfers between devices: 390 us -> 0 us
  blocking collectives: 291 us -> 0 us
  Pallas kernels: 0 us -> 161 us
  starting transfers between devices: 95.9 us -> 0 us
  matrix products: 30.2 us -> 0 us
  local copies, waits for them, and re-layouts: 34.5 us -> 9.39 us
  between operations: 14.3 us -> 0.65 us
    all_to_all x4 -> x0, waiting for transfers between devices: 260 us -> none  [the longest x1 176 us: body(): lax.all_to_all(pack(whole_dy), 'expert', split_axis=0, concat_axis=0, til...]
    all_gather x2 -> x0, blocking collectives: 218 us -> none  [the longest x1 140 us: body(): lax.all_gather(upstream, 'tensor', axis=1, tiled=True)]
    pallas_call x0 -> x1, Pallas kernels: none -> 161 us  [body(): pl.pallas_call(kernel, out_shape=out, in_specs=[vmem] * 7, out_specs=(vme...]
    reduce_scatter x1 -> x0, waiting for transfers between devices: 130 us -> none  [body(): lax.psum_scatter(dx_part.reshape(sources, capacity, width).astype(jnp.bfl...]
    all_to_all x4 -> x0, starting transfers between devices: 95.7 us -> none  [the longest x1 54.4 us: body(): lax.all_to_all(pack(whole_dy), 'expert', split_axis=0, concat_axis=0, til...]
    psum x1 -> x0, blocking collectives: 36.6 us -> none  [body(): lax.psum(partial_dp, 'tensor').astype(jnp.bfloat16)]
    all_to_all x1 -> x0, blocking collectives: 36.5 us -> none  [body(): lax.all_to_all(dp_rows, 'expert', split_axis=0, concat_axis=0, tiled=True)]
    dot_general x8 -> x0, matrix products: 30.2 us -> none  [contract(): lax.dot_general(left, right, (((left_dim,), (right_dim,)), ((), ())), pre...]
  transfers between devices with their start and end apart: 5 -> 0, of which waited for: 4 -> 0; matrix products, arithmetic and copies ran while one was open for 5% -> 0% of each run, Pallas kernels for 0% -> 0%
where the time goes in v1:
time: 172 us; the launch traced here: 171 us
  Pallas kernels  161 us (94%)
  local copies, waits for them, and re-layouts  9.39 us (5%)
    pallas_call x1, Pallas kernels, body(): pl.pallas_call(kernel, out_shape=out, in_specs=[vmem] * 7, out_specs=(vme...  161 us
    unnamed x12, local copies, waits for them, and re-layouts  7.97 us

profile of v1, /device:TPU:1, one launch (start us, length us, event | category | flops | bytes accessed | tf_op | source)
XLA Modules:
  0.0 171.1 jit_solution(2795894299062158191)
XLA Ops:
  0.6 0.0 copy-start.2
  0.6 1.4 copy.12.prob
  2.1 0.0 copy-done.2
  2.1 0.7 copy.13.ids
  2.8 161.1 %shard_map.110 = (bf16[128,256]{1,0:T(8,128)(2,1)}, bf16[128,6]{1,0:T(8,128)(2,1)}, bf16[1,176,2048]{2,1,0:T(8,128)(2,1)}, bf16[1,176,2048]{2,1,0:T(8,128)(2,1)}, bf16[1,176,2048]{2,1,0:T(8,128)(2,1)}) custom-call(bf16[128,256]{1,0:T(8,128)(2,1)} %tok.1, bf16[128,256]{1,0:T(8,128)(2,1)} %ups.1, bf16[128,6]{1,0:T(8,128)(2,1)} %copy.12.prob, ...), custom_call_target="tpu_custom_call" | custom-call | flops 5905580032 | bytes 8388608 | tf_op jit(solution)/shard_map/pallas_call | solution.py:355
  163.9 1.4 copy.14
  165.3 1.5 copy.19
  166.8 0.0 copy-start.1
  166.8 2.1 %copy.20 = bf16[1,176,2048]{2,1,0:T(8,128)(2,1)} copy(bf16[1,176,2048]{2,1,0:T(8,128)(2,1)} %get-tuple-element.17) | data formatting | bytes 1441792
  168.9 0.0 copy-done.1
  168.9 0.0 copy-start
  168.9 0.9 copy.21
  169.8 0.5 copy-done
  170.3 0.9 copy.22
Async XLA Ops:
  0.6 1.4 copy-start.2
  166.8 2.1 %copy-start.1 = (bf16[1,176,2048]{2,1,0:T(8,128)(2,1)S(1)}, bf16[1,176,2048]{2,1,0:T(8,128)(2,1)}, u32[]{:S(2)}) copy-start(bf16[1,176,2048]{2,1,0:T(8,128)(2,1)} %get-tuple-element.18) | copy-start | bytes 2162692
  168.9 1.4 copy-start

commit v2 on v1

--- a/solution.py
+++ b/solution.py
@@ -21,6 +21,7 @@
 META = 16
 WIDE = 2 * FS
 HALF = TOK // 2
+SUMS = 9
 
 
 def dot(a, b, ad=1, bd=0):
@@ -32,11 +33,12 @@
 
 
 def kernel(
-    tok, ups, prob, ids, wg, wu, wd,
-    gtok, gprob, ggate, gup, gdown,
+    tok, ups, prob, ids, wg_far, wu_far, wd_far,
+    gtok, gprob, ggate_far, gup_far, gdown_far,
+    wg, wu, wd, ggate, gup, gdown, s_in, s_out,
     held, ysend, wsend, rows_x, wrow, dau_t, ph_t, own, part_o, part_rl, buf_a, buf_b,
-    fsend, frecv, gsend, zrecv, dpx,
-    s_z, r_z, s_y, r_y, s_w, r_w, s_x, r_x, s_a, r_a, s_b, r_b, s_f, r_f, s_g, r_g, s_d, r_d,
+    fsend, frecv, gsend, zrecv, chain, dpx,
+    s_z, r_z, s_y, r_y, s_w, r_w, s_x, r_x, s_a, r_a, s_b, r_b, s_f, r_f, s_c, r_c, s_g, r_g, s_d, r_d,
 ):
     zl, zh = lax.axis_index("zl"), lax.axis_index("zh")
     x = lax.axis_index("x")
@@ -56,6 +58,17 @@
             src_ref=src, dst_ref=dst, send_sem=s_sem, recv_sem=r_sem,
             device_id=device, device_id_type=MESH,
         ).start()
+
+    loads = [
+        pltpu.make_async_copy(far.at[0], near, s_in.at[n])
+        for n, (far, near) in enumerate(((wg_far, wg), (wu_far, wu), (wd_far, wd)))
+    ]
+    stores = [
+        pltpu.make_async_copy(near, far.at[0], s_out.at[n])
+        for n, (near, far) in enumerate(((ggate, ggate_far), (gup, gup_far), (gdown, gdown_far)))
+    ]
+    for load in loads:
+        load.start()
 
     barrier = pltpu.get_barrier_semaphore()
     for d in range(1, NZ):
@@ -67,12 +80,11 @@
 
     row_id = lax.broadcasted_iota(jnp.int32, (TOK, TOK), 0)
     col_id = lax.broadcasted_iota(jnp.int32, (TOK, TOK), 1)
-    eye = (row_id == col_id).astype(F32).astype(BF16)
     earlier = (row_id < col_id).astype(F32).astype(BF16)
     held[0, 0:TOK, 0:FS] = tok[...]
     held[0, 0:TOK, FS:WIDE] = ups[...]
-    ids_t = dot(ids[...].astype(F32).astype(BF16), eye, 0, 0)
-    prob_t = dot(prob[...], eye, 0, 0)
+    ids_t = ids[...].astype(F32)
+    prob_t = prob[...].astype(F32)
     expert = lax.broadcasted_iota(jnp.int32, (ZL * YC, TOK), 0).astype(F32)
     named = jnp.zeros((ZL * YC, TOK), F32)
     for k in range(TOP):
@@ -198,9 +210,9 @@
                 f = features(slot, half)
                 xs = rows_x[slot, half, rows, 0:FS]
                 dys = rows_x[slot, half, rows, FS:WIDE]
-                a = a + dot(xs, wg[0, :, f], 1, 1)
-                u = u + dot(xs, wu[0, :, f], 1, 1)
-                g = g + dot(dys, wd[0, :, f], 1, 1)
+                a = a + dot(xs, wg[:, f], 1, 1)
+                u = u + dot(xs, wu[:, f], 1, 1)
+                g = g + dot(dys, wd[:, f], 1, 1)
         weight = wrow[rows, :].astype(F32)[:, 0:1]
         sig = jax.nn.sigmoid(a)
         act = a * sig
@@ -220,7 +232,7 @@
             for half in range(ZH):
                 f = features(slot, half)
                 to = slice(half * FS, half * FS + FS)
-                term = dot(d_a, wg[0, :, f]) + dot(d_u, wu[0, :, f])
+                term = dot(d_a, wg[:, f]) + dot(d_u, wu[:, f])
                 if slot == 0:
                     own[q, :, to] = term
                 elif slot == 3:
@@ -258,57 +270,101 @@
             theirs = pl.ds(pl.multiple_of(to * CAP, CAP), CAP)
             send(fsend.at[q, theirs, :], frecv.at[q, my_rows, :], s_f, r_f.at[q], at_yc(to))
 
-    def combine(p):
+    def combine(p, m):
         q = p - ZL
-        block, _ = source(p)
+        block, far = source(p)
+        near = 1 - far
         arrived(fsend.at[q, pl.ds(0, TOK - CAP), :], r_f.at[q])
         code, _ = routing(p)
         pick = spread(code, None).astype(BF16)
-        total = dot(pick, frecv[q, :, 0:WIDE], 0, 0).astype(BF16)
+        gsend[q, :, 0:TOK, :] = jnp.stack(
+            [dot(pick, frecv[q, :, h * FS : h * FS + FS], 0, 0) for h in range(ZH)]
+        ).astype(BF16)
         dp = frecv[q, :, WIDE : WIDE + TOK].astype(F32)
         dp_rows = jnp.zeros((META, TOK), F32)
         for k in range(TOP):
             one = jnp.sum(jnp.where(row_f == code[k : k + 1], dp, 0.0), axis=0, keepdims=True)
             dp_rows = jnp.where(line == k, one, dp_rows)
         for half in range(ZH):
-            gsend[q, half, 0:TOK, :] = total[:, half * FS : half * FS + FS]
             gsend[q, half, TOK : TOK + META, 0:TOK] = dp_rows.astype(BF16)
             gsend[q, half, TOK : TOK + META, TOK : 2 * TOK] = jnp.zeros((META, TOK), BF16)
 
-        @pl.when(q < ZL - 1)
-        def _():
-            for half in range(ZH):
-                to = block + half * ZL
-                send(gsend.at[q, half], zrecv.at[lax.rem(to + NZ - z, NZ)], s_g, r_g, at_z(to))
-
-        @pl.when(q == ZL - 1)
-        def _():
-            zrecv[0] = gsend[ZL - 1, zh]
-            send(gsend.at[ZL - 1, 1 - zh], zrecv.at[ZL], s_g, r_g, at_z(lax.rem(z + ZL, NZ)))
+        def place(to):
+            away = lax.rem(to + NZ - z, NZ)
+            return jnp.where(away < 5, away, away - 7)
+
+        @pl.when((m >= 2) & (m < 7))
+        def _():
+            arrived(chain.at[m], r_c.at[m])
+            gsend[q, far] = (gsend[q, far].astype(F32) + chain[m].astype(F32)).astype(BF16)
+
+        @pl.when(m == 7)
+        def _():
+            for n, half in ((8, far), (7, near)):
+                arrived(chain.at[n], r_c.at[n])
+                gsend[q, half] = (gsend[q, half].astype(F32) + chain[n].astype(F32)).astype(BF16)
+
+        @pl.when(m < 7)
+        def _():
+            step = jnp.where(lax.rem(m, 2) == 0, 1, NZ - 1)
+            send(gsend.at[q, far], chain.at[m + 2], s_c, r_c.at[m + 2], at_z(lax.rem(z + step, NZ)))
+
+        @pl.when(m == 7)
+        def _():
+            to = block + far * ZL
+            send(gsend.at[q, far], zrecv.at[place(to)], s_g, r_g, at_z(to))
+
+        @pl.when(m > 0)
+        def _():
+            to = block + near * ZL
+            send(gsend.at[q, near], zrecv.at[place(to)], s_g, r_g, at_z(to))
+
+        @pl.when(m == 0)
+        def _():
+            zrecv[0] = gsend[q, near]
 
     def weight_grads(slot):
         for half in range(ZH):
             f = features(slot, half)
             both = dot(dau_t[...], rows_x[slot, half, :, 0:FS])
-            ggate[0, :, f] = both[0:HID].astype(BF16)
-            gup[0, :, f] = both[HID : 2 * HID].astype(BF16)
-            gdown[0, :, f] = dot(ph_t[...], rows_x[slot, half, :, FS:WIDE]).astype(BF16)
+            ggate[:, f] = both[0:HID].astype(BF16)
+            gup[:, f] = both[HID : 2 * HID].astype(BF16)
+            gdown[:, f] = dot(ph_t[...], rows_x[slot, half, :, FS:WIDE]).astype(BF16)
+
+    def turn(j):
+        m = j - ZL
+        late = jnp.where(lax.rem(j, 2) == 1, jnp.maximum(14 - m, ZL), jnp.minimum(NZ - m, NZ - 1))
+        return jnp.where(j < ZL, j, late)
 
     def step(i, carry):
         def when(lag, least, act):
-            p = i - lag
-
-            @pl.when((p >= least) & (p < NZ))
+            j = i - lag
+
+            @pl.when((j >= least) & (j < NZ))
             def _():
-                act(p)
-
-        when(0, 0, take_in)
+                act(turn(j), *((j - ZL,) if act is combine else ()))
+
         when(1, 0, pass_on)
+
+        @pl.when((i > 0) & (i <= ZL))
+        def _():
+            take_in(2 * i - 1)
+
+        @pl.when(i < ZL)
+        def _():
+            take_in(2 * i)
+
         when(2, 0, relay)
         when(6, ZL, combine)
         when(5, ZL, send_back)
         when(4, ZL, add_relay)
         when(3, 0, all_here)
+
+        @pl.when(i == ZL)
+        def _():
+            for load in loads:
+                load.wait()
+
         when(3, ZL, compute)
 
         @pl.when(i >= NZ + 2)
@@ -318,11 +374,13 @@
         return carry
 
     lax.fori_loop(0, NZ + 6, step, 0)
-
-    arrived(zrecv.at[pl.ds(1, NZ - 1)], r_g)
+    for store in stores:
+        store.start()
+
+    arrived(zrecv.at[pl.ds(1, SUMS - 1)], r_g)
     total = jnp.zeros((TOK, FS), F32)
     dp = jnp.zeros((META, TOK), F32)
-    for s in range(NZ):
+    for s in range(SUMS):
         total = total + zrecv[s, 0:TOK, :].astype(F32)
         dp = dp + zrecv[s, TOK : TOK + META, 0:TOK].astype(F32)
     dpx[x] = dp
@@ -331,7 +389,10 @@
     gtok[...] = total.astype(BF16)
     arrived(dpx.at[pl.ds(0, NX - 1)], r_d)
     dp = (dpx[0] + dpx[1]) + (dpx[2] + dpx[3])
-    gprob[...] = dot(eye, dp.astype(BF16), 1, 1)[:, 0:TOP].astype(BF16)
+    gprob[...] = dp[0:TOP].astype(BF16)
+
+    for store in stores:
+        store.wait()
 
     arrived(held.at[pl.ds(0, NZ - 1)], s_z)
     arrived(ysend.at[:, pl.ds(0, TOK - CAP), :], s_y)
@@ -340,24 +401,40 @@
     arrived(part_o, s_a)
     arrived(part_rl, s_b)
     arrived(fsend.at[:, pl.ds(0, TOK - CAP), :], s_f)
-    arrived(zrecv.at[pl.ds(1, NZ - 1)], s_g)
+    arrived(zrecv.at[pl.ds(1, SUMS - 1)], s_g)
+    arrived(chain.at[pl.ds(2, 7)], s_c)
     arrived(dpx.at[pl.ds(0, NX - 1)], s_d)
+
+
+def hand_over(*refs):
+    sems = refs[-1]
+    copies = [
+        pltpu.make_async_copy(src, dst, sems.at[n])
+        for n, (src, dst) in enumerate(zip(refs[:5], refs[5:10]))
+    ]
+    for copy in copies:
+        copy.start()
+    for copy in copies:
+        copy.wait()
 
 
 def body(tokens, upstream, probs, expert_ids, gate_weight, up_weight, down_weight):
     vmem = pl.BlockSpec(memory_space=pltpu.VMEM)
+    anywhere = pl.BlockSpec(memory_space=pl.ANY)
     dma = pltpu.SemaphoreType.DMA
     width = NX * ZH * FS
     out = (
         jax.ShapeDtypeStruct((TOK, FS), BF16),
-        jax.ShapeDtypeStruct((TOK, TOP), BF16),
+        jax.ShapeDtypeStruct((TOP, TOK), BF16),
     ) + (jax.ShapeDtypeStruct((1, HID, width), BF16),) * 3
-    return pl.pallas_call(
+    results = pl.pallas_call(
         kernel,
         out_shape=out,
-        in_specs=[vmem] * 7,
-        out_specs=(vmem,) * 5,
-        scratch_shapes=[
+        in_specs=[vmem] * 4 + [anywhere] * 3,
+        out_specs=(vmem,) * 2 + (anywhere,) * 3,
+        scratch_shapes=[pltpu.VMEM((HID, width), BF16)] * 6
+        + [
+            dma((3,)), dma((3,)),
             pltpu.VMEM((NZ, TOK + META, WIDE), BF16),
             pltpu.VMEM((NZ, TOK, WIDE), BF16),
             pltpu.VMEM((ZL, TOK, TOK), BF16),
@@ -373,7 +450,8 @@
             pltpu.VMEM((ZL, TOK, WIDE + TOK), BF16),
             pltpu.VMEM((ZL, TOK, WIDE + TOK), BF16),
             pltpu.VMEM((ZL, ZH, TOK + META, FS), BF16),
-            pltpu.VMEM((NZ, TOK + META, FS), BF16),
+            pltpu.VMEM((SUMS, TOK + META, FS), BF16),
+            pltpu.VMEM((9, TOK + META, FS), BF16),
             pltpu.VMEM((NX, META, TOK), F32),
             dma, dma((NZ,)),
             dma, dma((NZ,)),
@@ -382,6 +460,7 @@
             dma, dma((ZL, 2)),
             dma, dma((ZL, 2)),
             dma, dma((ZL,)),
+            dma, dma((9,)),
             dma, dma,
             dma, dma,
         ],
@@ -391,7 +470,15 @@
         cost_estimate=pl.CostEstimate(
             flops=16 * ZL * TOK * HID * width, bytes_accessed=8 << 20, transcendentals=0
         ),
-    )(tokens, upstream, probs, expert_ids, gate_weight, up_weight, down_weight)
+    )(tokens, upstream, probs.T, expert_ids.T, gate_weight, up_weight, down_weight)
+    tokens_out, probs_out, *weights_out = pl.pallas_call(
+        hand_over,
+        out_shape=out,
+        in_specs=[vmem] * 5,
+        out_specs=(anywhere,) * 5,
+        scratch_shapes=[dma((5,))],
+    )(*results)
+    return (tokens_out, probs_out.T, *weights_out)
 
 
 def solution(mesh):

time: 172 us -> 159 us (0.924)
  local copies, waits for them, and re-layouts: 9.39 us -> 0 us
  Pallas kernels: 161 us -> 158 us
    unnamed x12 -> x0, local copies, waits for them, and re-layouts: 7.97 us -> none
    pallas_call x1 -> x2, Pallas kernels: 161 us -> 158 us  [the longest x1 155 us: body(): pl.pallas_call(kernel, out_shape=out, in_specs=[vmem] * 4 + [anywhere] *...]
where the time goes in v2:
time: 159 us
  Pallas kernels  158 us (99%)
    pallas_call x1, Pallas kernels, body(): pl.pallas_call(kernel, out_shape=out, in_specs=[vmem] * 4 + [anywhere] *...  155 us

profile of v2, /device:TPU:1, one launch (start us, length us, event | category | flops | bytes accessed | tf_op | source)
XLA Modules:
  0.0 158.9 jit_solution(11191733999565784820)
XLA Ops:
  0.6 155.3 %shard_map.110 = (bf16[128,256]{1,0:T(8,128)(2,1)}, bf16[6,128]{1,0:T(8,128)(2,1)}, bf16[1,176,2048]{2,1,0:T(8,128)(2,1)}, bf16[1,176,2048]{2,1,0:T(8,128)(2,1)}, bf16[1,176,2048]{2,1,0:T(8,128)(2,1)}) custom-call(bf16[128,256]{1,0:T(8,128)(2,1)} %tok.1, bf16[128,256]{1,0:T(8,128)(2,1)} %ups.1, bf16[6,128]{1,0:T(8,128)(2,1)} %bitcast.4, s32[6,128]{1,0:T(8,128)} %bitcast.3, ...), custom_call_target="tpu_custom_call" | custom-call | flops 5905580032 | bytes 8388608 | tf_op jit(solution)/shard_map/pallas_call | solution.py:430
  155.9 3.0 %shard_map.111 = (bf16[128,256]{1,0:T(8,128)(2,1)}, bf16[6,128]{1,0:T(8,128)(2,1)}, bf16[1,176,2048]{2,1,0:T(8,128)(2,1)}, bf16[1,176,2048]{2,1,0:T(8,128)(2,1)}, bf16[1,176,2048]{2,1,0:T(8,128)(2,1)}) custom-call(bf16[128,256]{1,0:T(8,128)(2,1)} %get-tuple-element.15.refs_0_, bf16[6,128]{1,0:T(8,128)(2,1)} %get-tuple-element.16.refs_1_, ...), custom_call_target="tpu_custom_call" | custom-call | tf_op jit(solution)/shard_map/pallas_call | solution.py:474

commit v3 on v2

--- a/solution.py
+++ b/solution.py
@@ -21,6 +21,7 @@
 META = 16
 WIDE = 2 * FS
 HALF = TOK // 2
+FAR_FIRST = (4, 3, 5, 2, 6, 1, 7)
 SUMS = 9
 
 
@@ -117,7 +118,8 @@
     row_f = row_id.astype(F32)
 
     def routing(p):
-        meta = held[p, TOK : TOK + META, :].astype(F32)
+        first = jnp.where(p < ZL, p, NZ - 1 - p)
+        meta = held[first, TOK : TOK + META, :].astype(F32)
         code = (meta[:, 0:TOK] - (zl * YC).astype(F32)) * CAP + meta[:, TOK : 2 * TOK]
         return code, meta[:, 2 * TOK : 3 * TOK]
 
@@ -129,20 +131,33 @@
         return total
 
     def take_in(p):
-        @pl.when(p > 0)
+        @pl.when((p > 0) & (p < ZL))
         def _():
             arrived(held.at[p], r_z.at[p])
 
+        @pl.when(p >= ZL)
+        def _():
+            arrived(held.at[p, pl.ds(0, TOK)], r_z.at[p])
+
         @pl.when(p == 0)
         def _():
-            send(held.at[0], held.at[1], s_z, r_z.at[1], at_z(lax.rem(z + 1, NZ)))
-            send(held.at[0], held.at[2], s_z, r_z.at[2], at_z(lax.rem(z + NZ - 1, NZ)))
-
-        @pl.when((p > 0) & (p < NZ - 2))
-        def _():
-            step = jnp.where(lax.rem(p, 2) == 1, 1, NZ - 1)
-            send(held.at[p], held.at[p + 2], s_z, r_z.at[p + 2], at_z(lax.rem(z + step, NZ)))
-
+            send(held.at[0], held.at[1], s_z.at[0], r_z.at[1], at_z(lax.rem(z + 1, NZ)))
+            send(held.at[0], held.at[2], s_z.at[0], r_z.at[2], at_z(lax.rem(z + NZ - 1, NZ)))
+
+        onward = at_z(lax.rem(z + jnp.where(lax.rem(p, 2) == 1, 1, NZ - 1), NZ))
+
+        @pl.when((p > 0) & (p < ZL - 2))
+        def _():
+            send(held.at[p], held.at[p + 2], s_z.at[0], r_z.at[p + 2], onward)
+
+        @pl.when((p >= ZL - 2) & (p < NZ - 2))
+        def _():
+            send(
+                held.at[p, pl.ds(0, TOK)], held.at[p + 2, pl.ds(0, TOK)],
+                s_z.at[1], r_z.at[p + 2], onward,
+            )
+
+    def pack(p):
         block, half = source(p)
         code, weights = routing(p)
         pick = spread(code, None).astype(BF16)
@@ -150,7 +165,7 @@
         mine = block_rows(block, CAP, me * CAP)
         my_rows = pl.ds(pl.multiple_of(me * CAP, CAP), CAP)
         rows_x[0, half, mine, :] = ysend[p, my_rows, :]
-        for d in range(1, YC):
+        for d in FAR_FIRST:
             to = lax.rem(me + d, YC)
             theirs = pl.ds(pl.multiple_of(to * CAP, CAP), CAP)
             send(ysend.at[p, theirs, :], rows_x.at[0, half, mine, :], s_y, r_y.at[p], at_yc(to))
@@ -161,7 +176,7 @@
             weight = jnp.sum(spread(code, weights), axis=1, keepdims=True)
             wsend[q] = jnp.broadcast_to(weight, (TOK, TOK)).astype(BF16)
             wrow[mine, :] = wsend[q, my_rows, :]
-            for d in range(1, YC):
+            for d in FAR_FIRST:
                 to = lax.rem(me + d, YC)
                 theirs = pl.ds(pl.multiple_of(to * CAP, CAP), CAP)
                 send(wsend.at[q, theirs, :], wrow.at[mine, :], s_w, r_w.at[q], at_yc(to))
@@ -217,8 +232,10 @@
         sig = jax.nn.sigmoid(a)
         act = a * sig
         hidden = (act * u).astype(BF16).astype(F32)
-        dp = jnp.sum(hidden * g, axis=1, keepdims=True)
-        fsend[q, :, WIDE : WIDE + TOK] = jnp.broadcast_to(dp, (TOK, TOK)).astype(BF16)
+        dp = jnp.sum((hidden * g).T, axis=0, keepdims=True)
+        dpx[q, x] = jnp.broadcast_to(dp, (8, TOK))
+        for d in range(1, NX):
+            send(dpx.at[q, x], dpx.at[q, x], s_d, r_d.at[q], {"x": lax.rem(x + d, NX)})
         dh = weight * g
         d_a = dh * u * sig * (1.0 + a * (1.0 - sig))
         d_u = dh * act
@@ -258,6 +275,9 @@
 
     def send_back(p):
         q = p - ZL
+        arrived(dpx.at[q, pl.ds(0, NX - 1)], r_d.at[q])
+        dp = (dpx[q, 0] + dpx[q, 1]) + (dpx[q, 2] + dpx[q, 3])
+        fsend[q, :, WIDE : WIDE + TOK] = jnp.broadcast_to(dp[0:1], (TOK, TOK)).T.astype(BF16)
         arrived(buf_b.at[0, q], r_b.at[q, 0])
         arrived(buf_b.at[1, q], r_b.at[q, 1])
         fsend[q, :, 0:WIDE] = (
@@ -265,7 +285,7 @@
         ).astype(BF16)
         my_rows = pl.ds(pl.multiple_of(me * CAP, CAP), CAP)
         frecv[q, my_rows, :] = fsend[q, my_rows, :]
-        for d in range(1, YC):
+        for d in FAR_FIRST:
             to = lax.rem(me + d, YC)
             theirs = pl.ds(pl.multiple_of(to * CAP, CAP), CAP)
             send(fsend.at[q, theirs, :], frecv.at[q, my_rows, :], s_f, r_f.at[q], at_yc(to))
@@ -344,15 +364,23 @@
             def _():
                 act(turn(j), *((j - ZL,) if act is combine else ()))
 
+        @pl.when((i > 0) & (i <= ZL))
+        def _():
+            take_in(2 * i - 1)
+
+        @pl.when(i < ZL)
+        def _():
+            take_in(2 * i)
+
         when(1, 0, pass_on)
 
-        @pl.when((i > 0) & (i <= ZL))
-        def _():
-            take_in(2 * i - 1)
-
-        @pl.when(i < ZL)
-        def _():
-            take_in(2 * i)
+        @pl.when((i < 2) | (i == ZL))
+        def _():
+            pack(turn(i))
+
+        @pl.when((i > 0) & (i != ZL - 1) & (i < NZ - 1))
+        def _():
+            pack(turn(i + 1))
 
         when(2, 0, relay)
         when(6, ZL, combine)
@@ -383,18 +411,13 @@
     for s in range(SUMS):
         total = total + zrecv[s, 0:TOK, :].astype(F32)
         dp = dp + zrecv[s, TOK : TOK + META, 0:TOK].astype(F32)
-    dpx[x] = dp
-    for d in range(1, NX):
-        send(dpx.at[x], dpx.at[x], s_d, r_d, {"x": lax.rem(x + d, NX)})
     gtok[...] = total.astype(BF16)
-    arrived(dpx.at[pl.ds(0, NX - 1)], r_d)
-    dp = (dpx[0] + dpx[1]) + (dpx[2] + dpx[3])
     gprob[...] = dp[0:TOP].astype(BF16)
-
     for store in stores:
         store.wait()
 
-    arrived(held.at[pl.ds(0, NZ - 1)], s_z)
+    arrived(held.at[pl.ds(0, ZL - 1)], s_z.at[0])
+    arrived(held.at[pl.ds(0, ZL), pl.ds(0, TOK)], s_z.at[1])
     arrived(ysend.at[:, pl.ds(0, TOK - CAP), :], s_y)
     arrived(wsend.at[:, pl.ds(0, TOK - CAP), :], s_w)
     arrived(rows_x.at[pl.ds(1, NX - 1)], s_x)
@@ -403,19 +426,20 @@
     arrived(fsend.at[:, pl.ds(0, TOK - CAP), :], s_f)
     arrived(zrecv.at[pl.ds(1, SUMS - 1)], s_g)
     arrived(chain.at[pl.ds(2, 7)], s_c)
-    arrived(dpx.at[pl.ds(0, NX - 1)], s_d)
+    arrived(dpx.at[:, pl.ds(0, NX - 1)], s_d)
 
 
 def hand_over(*refs):
-    sems = refs[-1]
-    copies = [
-        pltpu.make_async_copy(src, dst, sems.at[n])
-        for n, (src, dst) in enumerate(zip(refs[:5], refs[5:10]))
-    ]
-    for copy in copies:
-        copy.start()
-    for copy in copies:
-        copy.wait()
+    far, out, near, sems = refs[:5], refs[5:10], refs[10:15], refs[15]
+    loads = [pltpu.make_async_copy(far[n], near[n], sems.at[0, n]) for n in range(5)]
+    stores = [pltpu.make_async_copy(near[n], out[n], sems.at[1, n]) for n in range(5)]
+    for load in loads:
+        load.start()
+    for load, store in zip(loads, stores):
+        load.wait()
+        store.start()
+    for store in stores:
+        store.wait()
 
 
 def body(tokens, upstream, probs, expert_ids, gate_weight, up_weight, down_weight):
@@ -452,8 +476,8 @@
             pltpu.VMEM((ZL, ZH, TOK + META, FS), BF16),
             pltpu.VMEM((SUMS, TOK + META, FS), BF16),
             pltpu.VMEM((9, TOK + META, FS), BF16),
-            pltpu.VMEM((NX, META, TOK), F32),
-            dma, dma((NZ,)),
+            pltpu.VMEM((ZL, NX, 8, TOK), F32),
+            dma((2,)), dma((NZ,)),
             dma, dma((NZ,)),
             dma, dma((ZL,)),
             dma, dma((NZ, 4)),
@@ -462,7 +486,7 @@
             dma, dma((ZL,)),
             dma, dma((9,)),
             dma, dma,
-            dma, dma,
+            dma, dma((ZL,)),
         ],
         compiler_params=pltpu.CompilerParams(
             collective_id=0, has_side_effects=True, vmem_limit_bytes=56 * 1024 * 1024
@@ -474,9 +498,9 @@
     tokens_out, probs_out, *weights_out = pl.pallas_call(
         hand_over,
         out_shape=out,
-        in_specs=[vmem] * 5,
+        in_specs=[anywhere] * 5,
         out_specs=(anywhere,) * 5,
-        scratch_shapes=[dma((5,))],
+        scratch_shapes=[pltpu.VMEM(o.shape, o.dtype) for o in out] + [dma((2, 5))],
     )(*results)
     return (tokens_out, probs_out.T, *weights_out)
 

time: 159 us -> 155 us (0.975)
  Pallas kernels: 158 us -> 154 us
    pallas_call x1, Pallas kernels: 155 us -> 151 us  [body(): pl.pallas_call(kernel, out_shape=out, in_specs=[vmem] * 4 + [anywhere] *...]
where the time goes in v3:
time: 155 us; the launch traced here: 154 us
  Pallas kernels  154 us (99%)
    pallas_call x1, Pallas kernels, body(): pl.pallas_call(kernel, out_shape=out, in_specs=[vmem] * 4 + [anywhere] *...  151 us

profile of v3, /device:TPU:1, one launch (start us, length us, event | category | flops | bytes accessed | tf_op | source)
XLA Modules:
  0.0 154.4 jit_solution(18348937040703259395)
XLA Ops:
  0.6 151.2 %shard_map.110 = (bf16[128,256]{1,0:T(8,128)(2,1)}, bf16[6,128]{1,0:T(8,128)(2,1)}, bf16[1,176,2048]{2,1,0:T(8,128)(2,1)}, bf16[1,176,2048]{2,1,0:T(8,128)(2,1)}, bf16[1,176,2048]{2,1,0:T(8,128)(2,1)}) custom-call(bf16[128,256]{1,0:T(8,128)(2,1)} %tok.1, bf16[128,256]{1,0:T(8,128)(2,1)} %ups.1, bf16[6,128]{1,0:T(8,128)(2,1)} %bitcast.4, s32[6,128]{1,0:T(8,128)} %bitcast.3, ...), custom_call_target="tpu_custom_call" | custom-call | flops 5905580032 | bytes 8388608 | tf_op jit(solution)/shard_map/pallas_call | solution.py:454
  151.9 2.6 %shard_map.111 = (bf16[128,256]{1,0:T(8,128)(2,1)}, bf16[6,128]{1,0:T(8,128)(2,1)}, bf16[1,176,2048]{2,1,0:T(8,128)(2,1)}, bf16[1,176,2048]{2,1,0:T(8,128)(2,1)}, bf16[1,176,2048]{2,1,0:T(8,128)(2,1)}) custom-call(bf16[128,256]{1,0:T(8,128)(2,1)} %get-tuple-element.15.refs_0_, bf16[6,128]{1,0:T(8,128)(2,1)} %get-tuple-element.16.refs_1_, ...), custom_call_target="tpu_custom_call" | custom-call | tf_op jit(solution)/shard_map/pallas_call | solution.py:498

commit v4 on v3

--- a/solution.py
+++ b/solution.py
@@ -130,32 +130,46 @@
             total = total + jnp.where(row_f == code[k : k + 1], value, 0.0)
         return total
 
-    def take_in(p):
-        @pl.when((p > 0) & (p < ZL))
-        def _():
-            arrived(held.at[p], r_z.at[p])
+    def top(p):
+        return held.at[p, pl.ds(0, HALF)]
+
+    def rest(p, rows):
+        return held.at[p, pl.ds(HALF, rows)]
+
+    routed, bare = HALF + META, HALF
+
+    def onward(p):
+        return at_z(lax.rem(z + jnp.where(lax.rem(p, 2) == 1, 1, NZ - 1), NZ))
+
+    def take_top(p):
+        arrived(top(p), r_z.at[p, 0])
+
+        @pl.when(p < NZ - 2)
+        def _():
+            send(top(p), top(p + 2), s_z.at[0], r_z.at[p + 2, 0], onward(p))
+
+    def take_rest(p):
+        @pl.when(p < ZL)
+        def _():
+            arrived(rest(p, routed), r_z.at[p, 1])
 
         @pl.when(p >= ZL)
         def _():
-            arrived(held.at[p, pl.ds(0, TOK)], r_z.at[p])
-
-        @pl.when(p == 0)
-        def _():
-            send(held.at[0], held.at[1], s_z.at[0], r_z.at[1], at_z(lax.rem(z + 1, NZ)))
-            send(held.at[0], held.at[2], s_z.at[0], r_z.at[2], at_z(lax.rem(z + NZ - 1, NZ)))
-
-        onward = at_z(lax.rem(z + jnp.where(lax.rem(p, 2) == 1, 1, NZ - 1), NZ))
-
-        @pl.when((p > 0) & (p < ZL - 2))
-        def _():
-            send(held.at[p], held.at[p + 2], s_z.at[0], r_z.at[p + 2], onward)
+            arrived(rest(p, bare), r_z.at[p, 1])
+
+        @pl.when(p < ZL - 2)
+        def _():
+            send(rest(p, routed), rest(p + 2, routed), s_z.at[1], r_z.at[p + 2, 1], onward(p))
 
         @pl.when((p >= ZL - 2) & (p < NZ - 2))
         def _():
-            send(
-                held.at[p, pl.ds(0, TOK)], held.at[p + 2, pl.ds(0, TOK)],
-                s_z.at[1], r_z.at[p + 2], onward,
-            )
+            send(rest(p, bare), rest(p + 2, bare), s_z.at[2], r_z.at[p + 2, 1], onward(p))
+
+    def begin():
+        for p, place in ((1, z + 1), (2, z + NZ - 1)):
+            send(top(0), top(p), s_z.at[0], r_z.at[p, 0], at_z(lax.rem(place, NZ)))
+        for p, place in ((1, z + 1), (2, z + NZ - 1)):
+            send(rest(0, routed), rest(p, routed), s_z.at[1], r_z.at[p, 1], at_z(lax.rem(place, NZ)))
 
     def pack(p):
         block, half = source(p)
@@ -297,32 +311,31 @@
         arrived(fsend.at[q, pl.ds(0, TOK - CAP), :], r_f.at[q])
         code, _ = routing(p)
         pick = spread(code, None).astype(BF16)
-        gsend[q, :, 0:TOK, :] = jnp.stack(
-            [dot(pick, frecv[q, :, h * FS : h * FS + FS], 0, 0) for h in range(ZH)]
-        ).astype(BF16)
         dp = frecv[q, :, WIDE : WIDE + TOK].astype(F32)
         dp_rows = jnp.zeros((META, TOK), F32)
         for k in range(TOP):
             one = jnp.sum(jnp.where(row_f == code[k : k + 1], dp, 0.0), axis=0, keepdims=True)
             dp_rows = jnp.where(line == k, one, dp_rows)
-        for half in range(ZH):
+
+        def gather(half):
+            features_of = pl.ds(pl.multiple_of(half * FS, FS), FS)
+            gsend[q, half, 0:TOK, :] = dot(pick, frecv[q, :, features_of], 0, 0).astype(BF16)
             gsend[q, half, TOK : TOK + META, 0:TOK] = dp_rows.astype(BF16)
             gsend[q, half, TOK : TOK + META, TOK : 2 * TOK] = jnp.zeros((META, TOK), BF16)
+
+        gather(far)
 
         def place(to):
             away = lax.rem(to + NZ - z, NZ)
             return jnp.where(away < 5, away, away - 7)
 
+        def add(half, n):
+            arrived(chain.at[n], r_c.at[n])
+            gsend[q, half] = (gsend[q, half].astype(F32) + chain[n].astype(F32)).astype(BF16)
+
         @pl.when((m >= 2) & (m < 7))
         def _():
-            arrived(chain.at[m], r_c.at[m])
-            gsend[q, far] = (gsend[q, far].astype(F32) + chain[m].astype(F32)).astype(BF16)
-
-        @pl.when(m == 7)
-        def _():
-            for n, half in ((8, far), (7, near)):
-                arrived(chain.at[n], r_c.at[n])
-                gsend[q, half] = (gsend[q, half].astype(F32) + chain[n].astype(F32)).astype(BF16)
+            add(far, m)
 
         @pl.when(m < 7)
         def _():
@@ -331,8 +344,15 @@
 
         @pl.when(m == 7)
         def _():
+            add(far, 8)
             to = block + far * ZL
             send(gsend.at[q, far], zrecv.at[place(to)], s_g, r_g, at_z(to))
+
+        gather(near)
+
+        @pl.when(m == 7)
+        def _():
+            add(near, 7)
 
         @pl.when(m > 0)
         def _():
@@ -351,9 +371,14 @@
             gup[:, f] = both[HID : 2 * HID].astype(BF16)
             gdown[:, f] = dot(ph_t[...], rows_x[slot, half, :, FS:WIDE]).astype(BF16)
 
+    def rank(j):
+        m = j - ZL
+        return jnp.where(m < 2, 1 - m, m)
+
     def turn(j):
-        m = j - ZL
+        m = rank(j)
         late = jnp.where(lax.rem(j, 2) == 1, jnp.maximum(14 - m, ZL), jnp.minimum(NZ - m, NZ - 1))
+        late = jnp.where(m == 0, NZ - 1, jnp.where(m == 1, NZ - 3, late))
         return jnp.where(j < ZL, j, late)
 
     def step(i, carry):
@@ -362,29 +387,32 @@
 
             @pl.when((j >= least) & (j < NZ))
             def _():
-                act(turn(j), *((j - ZL,) if act is combine else ()))
-
-        @pl.when((i > 0) & (i <= ZL))
-        def _():
-            take_in(2 * i - 1)
-
-        @pl.when(i < ZL)
-        def _():
-            take_in(2 * i)
-
+                act(turn(j), *((rank(j),) if act is combine else ()))
+
+        def both(act):
+            @pl.when((i > 0) & (i <= ZL))
+            def _():
+                act(2 * i - 1)
+
+            @pl.when((i > 0) & (i < ZL))
+            def _():
+                act(2 * i)
+
+        both(take_top)
+        when(6, ZL, combine)
         when(1, 0, pass_on)
-
-        @pl.when((i < 2) | (i == ZL))
+        both(take_rest)
+
+        @pl.when(i < 2)
         def _():
             pack(turn(i))
 
-        @pl.when((i > 0) & (i != ZL - 1) & (i < NZ - 1))
+        @pl.when((i > 0) & (i < NZ - 1))
         def _():
             pack(turn(i + 1))
 
+        when(5, ZL, send_back)
         when(2, 0, relay)
-        when(6, ZL, combine)
-        when(5, ZL, send_back)
         when(4, ZL, add_relay)
         when(3, 0, all_here)
 
@@ -401,6 +429,7 @@
 
         return carry
 
+    begin()
     lax.fori_loop(0, NZ + 6, step, 0)
     for store in stores:
         store.start()
@@ -416,8 +445,9 @@
     for store in stores:
         store.wait()
 
-    arrived(held.at[pl.ds(0, ZL - 1)], s_z.at[0])
-    arrived(held.at[pl.ds(0, ZL), pl.ds(0, TOK)], s_z.at[1])
+    arrived(held.at[pl.ds(0, NZ - 1), pl.ds(0, HALF)], s_z.at[0])
+    arrived(held.at[pl.ds(0, ZL - 1), pl.ds(HALF, routed)], s_z.at[1])
+    arrived(held.at[pl.ds(0, ZL), pl.ds(HALF, bare)], s_z.at[2])
     arrived(ysend.at[:, pl.ds(0, TOK - CAP), :], s_y)
     arrived(wsend.at[:, pl.ds(0, TOK - CAP), :], s_w)
     arrived(rows_x.at[pl.ds(1, NX - 1)], s_x)
@@ -477,7 +507,7 @@
             pltpu.VMEM((SUMS, TOK + META, FS), BF16),
             pltpu.VMEM((9, TOK + META, FS), BF16),
             pltpu.VMEM((ZL, NX, 8, TOK), F32),
-            dma((2,)), dma((NZ,)),
+            dma((3,)), dma((NZ, 2)),
             dma, dma((NZ,)),
             dma, dma((ZL,)),
             dma, dma((NZ, 4)),

time: 155 us -> 152 us (0.981)
  Pallas kernels: 154 us -> 151 us
    pallas_call x1, Pallas kernels: 151 us -> 148 us  [body(): pl.pallas_call(kernel, out_shape=out, in_specs=[vmem] * 4 + [anywhere] *...]
where the time goes in v4:
time: 152 us; the launch traced here: 151 us
  Pallas kernels  151 us (99%)
    pallas_call x1, Pallas kernels, body(): pl.pallas_call(kernel, out_shape=out, in_specs=[vmem] * 4 + [anywhere] *...  148 us

profile of v4, /device:TPU:1, one launch (start us, length us, event | category | flops | bytes accessed | tf_op | source)
XLA Modules:
  0.0 151.3 jit_solution(14475198421116667764)
XLA Ops:
  0.6 148.1 %shard_map.110 = (bf16[128,256]{1,0:T(8,128)(2,1)}, bf16[6,128]{1,0:T(8,128)(2,1)}, bf16[1,176,2048]{2,1,0:T(8,128)(2,1)}, bf16[1,176,2048]{2,1,0:T(8,128)(2,1)}, bf16[1,176,2048]{2,1,0:T(8,128)(2,1)}) custom-call(bf16[128,256]{1,0:T(8,128)(2,1)} %tok.1, bf16[128,256]{1,0:T(8,128)(2,1)} %ups.1, bf16[6,128]{1,0:T(8,128)(2,1)} %bitcast.4, s32[6,128]{1,0:T(8,128)} %bitcast.3, ...), custom_call_target="tpu_custom_call" | custom-call | flops 5905580032 | bytes 8388608 | tf_op jit(solution)/shard_map/pallas_call | solution.py:484
  148.8 2.6 %shard_map.111 = (bf16[128,256]{1,0:T(8,128)(2,1)}, bf16[6,128]{1,0:T(8,128)(2,1)}, bf16[1,176,2048]{2,1,0:T(8,128)(2,1)}, bf16[1,176,2048]{2,1,0:T(8,128)(2,1)}, bf16[1,176,2048]{2,1,0:T(8,128)(2,1)}) custom-call(bf16[128,256]{1,0:T(8,128)(2,1)} %get-tuple-element.15.refs_0_, bf16[6,128]{1,0:T(8,128)(2,1)} %get-tuple-element.16.refs_1_, ...), custom_call_target="tpu_custom_call" | custom-call | tf_op jit(solution)/shard_map/pallas_call | solution.py:528

commit v5 on v4

--- a/solution.py
+++ b/solution.py
@@ -197,29 +197,33 @@
 
     def pass_on(p):
         block, half = source(p)
-        rows = block_rows(block)
         arrived(ysend.at[p, pl.ds(0, TOK - CAP), :], r_y.at[p])
 
         @pl.when(p >= ZL)
         def _():
             arrived(wsend.at[p - ZL, pl.ds(0, TOK - CAP), :], r_w.at[p - ZL])
 
-        send(rows_x.at[0, half, rows, :], rows_x.at[1, half, rows, :], s_x, r_x.at[p, 0], right)
-        send(rows_x.at[0, half, rows, :], rows_x.at[2, half, rows, :], s_x, r_x.at[p, 1], left)
+        low, high = block_rows(block, HALF), block_rows(block, HALF, HALF)
+        send(rows_x.at[0, half, low, :], rows_x.at[1, half, low, :], s_x, r_x.at[p, 0], right)
+        send(rows_x.at[0, half, high, :], rows_x.at[2, half, high, :], s_x, r_x.at[p, 1], left)
+        send(rows_x.at[0, half, high, :], rows_x.at[1, half, high, :], s_x, r_x.at[p, 4], right)
+        send(rows_x.at[0, half, low, :], rows_x.at[2, half, low, :], s_x, r_x.at[p, 5], left)
 
     def relay(p):
         block, half = source(p)
-        rows = block_rows(block)
         low, high = block_rows(block, HALF), block_rows(block, HALF, HALF)
-        arrived(rows_x.at[1, half, rows, :], r_x.at[p, 0])
+        arrived(rows_x.at[1, half, low, :], r_x.at[p, 0])
         send(rows_x.at[1, half, low, :], rows_x.at[3, half, low, :], s_x, r_x.at[p, 2], right)
-        arrived(rows_x.at[2, half, rows, :], r_x.at[p, 1])
+        arrived(rows_x.at[2, half, high, :], r_x.at[p, 1])
         send(rows_x.at[2, half, high, :], rows_x.at[3, half, high, :], s_x, r_x.at[p, 3], left)
 
     def all_here(p):
         block, half = source(p)
-        arrived(rows_x.at[3, half, block_rows(block, HALF), :], r_x.at[p, 2])
-        arrived(rows_x.at[3, half, block_rows(block, HALF, HALF), :], r_x.at[p, 3])
+        low, high = block_rows(block, HALF), block_rows(block, HALF, HALF)
+        arrived(rows_x.at[1, half, high, :], r_x.at[p, 4])
+        arrived(rows_x.at[2, half, low, :], r_x.at[p, 5])
+        arrived(rows_x.at[3, half, low, :], r_x.at[p, 2])
+        arrived(rows_x.at[3, half, high, :], r_x.at[p, 3])
 
     def features(slot, half):
         shift = (0, 3, 1, 2)[slot] if isinstance(slot, int) else jnp.where(
@@ -510,7 +514,7 @@
             dma((3,)), dma((NZ, 2)),
             dma, dma((NZ,)),
             dma, dma((ZL,)),
-            dma, dma((NZ, 4)),
+            dma, dma((NZ, 6)),
             dma, dma((ZL, 2)),
             dma, dma((ZL, 2)),
             dma, dma((ZL,)),

time: 152 us -> 152 us (level)
  no operation moved by 1% of the time
where the time goes in v5:
time: 152 us; the launch traced here: 151 us
  Pallas kernels  151 us (99%)
    pallas_call x1, Pallas kernels, body(): pl.pallas_call(kernel, out_shape=out, in_specs=[vmem] * 4 + [anywhere] *...  148 us

profile of v5, /device:TPU:1, one launch (start us, length us, event | category | flops | bytes accessed | tf_op | source)
XLA Modules:
  0.0 151.4 jit_solution(17433668736389554557)
XLA Ops:
  0.6 148.1 %shard_map.110 = (bf16[128,256]{1,0:T(8,128)(2,1)}, bf16[6,128]{1,0:T(8,128)(2,1)}, bf16[1,176,2048]{2,1,0:T(8,128)(2,1)}, bf16[1,176,2048]{2,1,0:T(8,128)(2,1)}, bf16[1,176,2048]{2,1,0:T(8,128)(2,1)}) custom-call(bf16[128,256]{1,0:T(8,128)(2,1)} %tok.1, bf16[128,256]{1,0:T(8,128)(2,1)} %ups.1, bf16[6,128]{1,0:T(8,128)(2,1)} %bitcast.4, s32[6,128]{1,0:T(8,128)} %bitcast.3, ...), custom_call_target="tpu_custom_call" | custom-call | flops 5905580032 | bytes 8388608 | tf_op jit(solution)/shard_map/pallas_call | solution.py:488
  148.8 2.6 %shard_map.111 = (bf16[128,256]{1,0:T(8,128)(2,1)}, bf16[6,128]{1,0:T(8,128)(2,1)}, bf16[1,176,2048]{2,1,0:T(8,128)(2,1)}, bf16[1,176,2048]{2,1,0:T(8,128)(2,1)}, bf16[1,176,2048]{2,1,0:T(8,128)(2,1)}) custom-call(bf16[128,256]{1,0:T(8,128)(2,1)} %get-tuple-element.15.refs_0_, bf16[6,128]{1,0:T(8,128)(2,1)} %get-tuple-element.16.refs_1_, ...), custom_call_target="tpu_custom_call" | custom-call | tf_op jit(solution)/shard_map/pallas_call | solution.py:532
